TPU v7x, 32 devices: a whole 2x2x4 slice. The times are simulated.
32 devices in a mesh: dp: 8 (over z, y), tensor: 4 (over x, core).
Axes of the slice: x: 2, y: 2, z: 4, core: 2. Of those that a mesh axis runs over, the one named last changes fastest.
Arguments:
- tokens: bfloat16 [8192, 1280], P(('dp', 'tensor')), may hold values from -6 to 6
- lengths: int32 [8], P('dp'), may hold values from 200 to 1024, as said below
- gain_one: float32 [1280], replicated, may hold values from 0.5 to 1.5
- shift_one: float32 [1280], replicated, may hold values from -1.75 to 1.75
- weight_in: bfloat16 [1280, 3, 1280], P(None, None, 'tensor'), may hold values from -0.15625 to 0.15625
- bias_in: float32 [2, 1280], P(None, 'tensor'), may hold values from -3 to 3
- weight_out: bfloat16 [1280, 1280], P('tensor'), may hold values from -1 to 1
- bias_out: float32 [1280], replicated, may hold values from -1.75 to 1.75
- gain_two: float32 [1280], replicated, may hold values from 0.5 to 1.5
- shift_two: float32 [1280], replicated, may hold values from -1.75 to 1.75
- weight_up: bfloat16 [1280, 5120], P(None, 'tensor'), may hold values from -0.15625 to 0.15625
- bias_up: float32 [5120], P('tensor'), may hold values from -3 to 3
- weight_down: bfloat16 [5120, 1280], P('tensor'), may hold values from -0.078125 to 0.078125
- bias_down: float32 [1280], replicated, may hold values from -1.75 to 1.75
- cotangent: bfloat16 [8192, 1280], P(('dp', 'tensor')), may hold values from -6 to 6
Outputs:
- layer_output: float32 [8192, 1280], P(('dp', 'tensor'))
- grad_tokens: float32 [8192, 1280], P(('dp', 'tensor'))
- grad_gain_one: float32 [1280], replicated
- grad_shift_one: float32 [1280], replicated
- grad_weight_in: float32 [1280, 3, 1280], P(None, None, 'tensor')
- grad_bias_in: float32 [2, 1280], P(None, 'tensor')
- grad_weight_out: float32 [1280, 1280], P('tensor')
- grad_bias_out: float32 [1280], replicated
- grad_gain_two: float32 [1280], replicated
- grad_shift_two: float32 [1280], replicated
- grad_weight_up: float32 [1280, 5120], P(None, 'tensor')
- grad_bias_up: float32 [5120], P('tensor')
- grad_weight_down: float32 [5120, 1280], P('tensor')
- grad_bias_down: float32 [1280], replicated
Inputs may be any that keep to these rules, and one draw needn't show every extreme that they name: Sentence s uses slots 0 to lengths[s] - 1; some sentence uses all 1024 slots and some uses the fewest allowed.
All inputs are finite; a program needn't handle non-finite values.
Results may differ from a plain program's by a relative error of at most 0.011.
Values may be sent and summed in bfloat16 or wider, within the bound.
A program may use at most 128 MiB of HBM per device.

v0:
```python
import jax
import jax.numpy as jnp
from jax import lax
from jax.sharding import PartitionSpec as P

HD = 64
LEN = 1024


def normalize(rows, gain, shift):
    centre = rows - jnp.mean(rows, axis=-1, keepdims=True)
    spread = jnp.mean(centre * centre, axis=-1, keepdims=True)
    return centre * lax.rsqrt(spread + 1e-05) * gain + shift


def masked_scores(query_block, key_seq, length):
    scores = jnp.einsum(
        "qhd,khd->hqk", query_block, key_seq, preferred_element_type=jnp.float32
    ) * HD ** (-0.5)
    valid = jnp.arange(LEN) < length
    return jnp.where(valid[None, None, :], scores, -1e30)


def forward_block(query_block, key_seq, value_seq, length):
    masked = masked_scores(query_block, key_seq, length)
    top = jnp.max(masked, axis=-1, keepdims=True)
    weights = jnp.exp(masked - top)
    total = jnp.sum(weights, axis=-1, keepdims=True)
    probs = (weights / total).astype(jnp.bfloat16)
    context = jnp.einsum("hqk,khd->qhd", probs, value_seq, preferred_element_type=jnp.float32)
    return (context, top[..., 0] + jnp.log(total[..., 0]))


def forward_sequence(item):
    query_seq, key_seq, value_seq, length = item
    return lax.map(
        lambda query_block: forward_block(query_block, key_seq, value_seq, length), query_seq
    )


def backward_sequence(item):
    query_seq, key_seq, value_seq, grad_seq, log_seq, length = item

    def step(carry, inner):
        key_total, value_total = carry
        query_block, grad_block, log_block = inner
        masked = masked_scores(query_block, key_seq, length)
        probs = jnp.exp(masked - log_block[..., None])
        grad_probs = jnp.einsum(
            "qhd,khd->hqk", grad_block, value_seq, preferred_element_type=jnp.float32
        )
        inner_sum = jnp.sum(grad_probs * probs, axis=-1, keepdims=True)
        grad_scores = (probs * (grad_probs - inner_sum)).astype(jnp.bfloat16)
        query_grad = (
            jnp.einsum("hqk,khd->qhd", grad_scores, key_seq, preferred_element_type=jnp.float32)
            * HD ** (-0.5)
        ).astype(jnp.bfloat16)
        key_total = key_total + jnp.einsum(
            "hqk,qhd->khd", grad_scores, query_block, preferred_element_type=jnp.float32
        ) * HD ** (-0.5)
        value_total = value_total + jnp.einsum(
            "hqk,qhd->khd",
            probs.astype(jnp.bfloat16),
            grad_block,
            preferred_element_type=jnp.float32,
        )
        return ((key_total, value_total), query_grad)

    zero_state = jnp.zeros(key_seq.shape, jnp.float32)
    (key_total, value_total), query_grads = lax.scan(
        step, (zero_state, zero_state), (query_seq, grad_seq, log_seq)
    )
    return (query_grads, key_total.astype(jnp.bfloat16), value_total.astype(jnp.bfloat16))


def local(
    tokens,
    lengths,
    gain_one,
    shift_one,
    weight_in,
    bias_in,
    weight_out,
    bias_out,
    gain_two,
    shift_two,
    weight_up,
    bias_up,
    weight_down,
    bias_down,
    cotangent,
):
    sentences = lengths.shape[0]
    width = weight_in.shape[2]
    heads = width // HD
    block_rows = min(512, LEN)
    blocks = LEN // block_rows
    group_rows = sentences * LEN
    query_shape = (sentences, blocks, block_rows, heads, HD)
    key_shape = (sentences, LEN, heads, HD)
    rows_in = tokens.astype(jnp.float32)
    first_local = normalize(rows_in, gain_one, shift_one).astype(jnp.bfloat16)
    first = lax.all_gather(first_local, "tensor", axis=0, tiled=True)
    mixed = jnp.einsum("rd,dcw->rcw", first, weight_in, preferred_element_type=jnp.float32)
    query_rows = (mixed[:, 0] + bias_in[0]).astype(jnp.bfloat16).reshape(query_shape)
    key_rows = mixed[:, 1].astype(jnp.bfloat16).reshape(key_shape)
    value_rows = (mixed[:, 2] + bias_in[1]).astype(jnp.bfloat16).reshape(key_shape)
    context, log_totals = lax.map(forward_sequence, (query_rows, key_rows, value_rows, lengths))
    context_rows = context.reshape(group_rows, width).astype(jnp.bfloat16)
    middle = rows_in + (
        lax.psum_scatter(
            jnp.dot(context_rows, weight_out, preferred_element_type=jnp.float32),
            "tensor",
            scatter_dimension=0,
            tiled=True,
        )
        + bias_out
    )
    second_local = normalize(middle, gain_two, shift_two).astype(jnp.bfloat16)
    second = lax.all_gather(second_local, "tensor", axis=0, tiled=True)
    hidden = jnp.dot(second, weight_up, preferred_element_type=jnp.float32) + bias_up
    active = jax.nn.gelu(hidden, approximate=False).astype(jnp.bfloat16)
    layer_output = (
        middle
        + lax.psum_scatter(
            jnp.dot(active, weight_down, preferred_element_type=jnp.float32).astype(jnp.bfloat16),
            "tensor",
            scatter_dimension=0,
            tiled=True,
        ).astype(jnp.float32)
        + bias_down
    )
    grad_out = cotangent.astype(jnp.float32)
    grad_bias_down = jnp.sum(grad_out, axis=0)
    cot_group = lax.all_gather(cotangent, "tensor", axis=0, tiled=True)
    grad_weight_down = jnp.einsum(
        "rf,rd->fd", active, cot_group, preferred_element_type=jnp.float32
    )
    grad_active = jnp.einsum(
        "rd,fd->rf", cot_group, weight_down, preferred_element_type=jnp.float32
    )
    before_gelu = jnp.dot(second, weight_up, preferred_element_type=jnp.float32) + bias_up
    unused, gelu_pull = jax.vjp(lambda value: jax.nn.gelu(value, approximate=False), before_gelu)
    grad_hidden = gelu_pull(grad_active)[0].astype(jnp.bfloat16)
    grad_weight_up = jnp.einsum(
        "rd,rf->df", second, grad_hidden, preferred_element_type=jnp.float32
    )
    grad_bias_up = jnp.sum(grad_hidden.astype(jnp.float32), axis=0)
    grad_second = lax.psum_scatter(
        jnp.einsum("rf,df->rd", grad_hidden, weight_up, preferred_element_type=jnp.float32),
        "tensor",
        scatter_dimension=0,
        tiled=True,
    )
    unused_two, second_pull = jax.vjp(normalize, middle, gain_two, shift_two)
    middle_part, grad_gain_two, grad_shift_two = second_pull(grad_second)
    grad_middle = grad_out + middle_part
    grad_branch = grad_middle.astype(jnp.bfloat16)
    grad_bias_out = jnp.sum(grad_branch.astype(jnp.float32), axis=0)
    branch_group = lax.all_gather(grad_branch, "tensor", axis=0, tiled=True)
    grad_weight_out = jnp.einsum(
        "rw,rd->wd", context_rows, branch_group, preferred_element_type=jnp.float32
    )
    grad_context = jnp.einsum(
        "rd,wd->rw", branch_group, weight_out, preferred_element_type=jnp.float32
    ).astype(jnp.bfloat16)
    query_grads, key_grads, value_grads = lax.map(
        backward_sequence,
        (query_rows, key_rows, value_rows, grad_context.reshape(query_shape), log_totals, lengths),
    )
    query_flat = query_grads.reshape(group_rows, width)
    value_flat = value_grads.reshape(group_rows, width)
    grad_mixed = jnp.stack([query_flat, key_grads.reshape(group_rows, width), value_flat], axis=1)
    grad_weight_in = jnp.einsum(
        "rd,rcw->dcw", first, grad_mixed, preferred_element_type=jnp.float32
    )
    grad_bias_in = jnp.stack(
        [
            jnp.sum(query_flat.astype(jnp.float32), axis=0),
            jnp.sum(value_flat.astype(jnp.float32), axis=0),
        ]
    )
    grad_first = lax.psum_scatter(
        jnp.einsum("rcw,dcw->rd", grad_mixed, weight_in, preferred_element_type=jnp.float32),
        "tensor",
        scatter_dimension=0,
        tiled=True,
    )
    unused_one, first_pull = jax.vjp(normalize, rows_in, gain_one, shift_one)
    rows_part, grad_gain_one, grad_shift_one = first_pull(grad_first)
    grad_tokens = grad_middle + rows_part
    (
        grad_weight_in,
        grad_bias_in,
        grad_weight_out,
        grad_weight_up,
        grad_bias_up,
        grad_weight_down,
    ) = lax.psum(
        (
            grad_weight_in,
            grad_bias_in,
            grad_weight_out,
            grad_weight_up,
            grad_bias_up,
            grad_weight_down,
        ),
        "dp",
    )
    grad_gain_one, grad_shift_one, grad_bias_out, grad_gain_two, grad_shift_two, grad_bias_down = (
        lax.psum(
            (
                grad_gain_one,
                grad_shift_one,
                grad_bias_out,
                grad_gain_two,
                grad_shift_two,
                grad_bias_down,
            ),
            ("dp", "tensor"),
        )
    )
    return (
        layer_output,
        grad_tokens,
        grad_gain_one,
        grad_shift_one,
        grad_weight_in,
        grad_bias_in,
        grad_weight_out,
        grad_bias_out,
        grad_gain_two,
        grad_shift_two,
        grad_weight_up,
        grad_bias_up,
        grad_weight_down,
        grad_bias_down,
    )


def solution(mesh):
    placed = (
        P(("dp", "tensor"), None),
        P("dp"),
        P(),
        P(),
        P(None, None, "tensor"),
        P(None, "tensor"),
        P("tensor", None),
        P(),
        P(),
        P(),
        P(None, "tensor"),
        P("tensor"),
        P("tensor", None),
        P(),
        P(("dp", "tensor"), None),
    )
    return jax.shard_map(
        local,
        mesh=mesh,
        in_specs=placed,
        out_specs=(
            P(("dp", "tensor"), None),
            P(("dp", "tensor"), None),
            P(),
            P(),
            P(None, None, "tensor"),
            P(None, "tensor"),
            P("tensor", None),
            P(),
            P(),
            P(),
            P(None, "tensor"),
            P("tensor"),
            P("tensor", None),
            P(),
        ),
        check_vma=False,
    )
```

profile of v0, /device:TPU:0, one launch (start us, length us, event | category | flops | bytes accessed | tf_op | source)
XLA Modules:
  0.0 1077.7 jit_solution(7965360894861383481)
XLA Ops:
  13.8 28.2 %all-gather.5.cloned.1.call-done = bf16[1024,1280]{1,0:T(8,128)(2,1)} async-done(((bf16[256,1280]{1,0:T(8,128)(2,1)}), bf16[1024,1280]{1,0:T(8,128)(2,1)}) %all-gather.5.cloned.1.call-update) | async-done | bytes 2621456 | tf_op jit(solution)/shard_map/all_gather | solution.py:103
  41.9 5.2 fusion.50
  49.7 3.2 squeeze.48
  52.9 2.5 fusion.63
  56.4 20.4 %while.47 = (s32[]{:T(128)}, bf16[2,512,5,64]{1,3,2,0:T(8,128)(2,1)}, f32[2,5,512]{2,1,0:T(8,128)S(1)}, s32[]{:T(128)}, bf16[2,512,5,64]{1,3,2,0:T(8,128)(2,1)},...) while((s32[]{:T(128)}, bf16[2,512,5,64]{1,3,2,0:T(8,128)(2,1)}, ...), condition=%wide.region_5.6_spmd, body=%wide.region_2.5_spmd.sunk | while | flops 702544384 | bytes 36478072 | solution.py:36
  57.1 2.9 fusion.129
  60.0 2.5 fusion.130
  62.5 4.1 fusion.131
  67.3 2.9 fusion.129
  70.1 2.5 fusion.130
  72.7 4.1 fusion.131
  79.6 3.9 fusion.76
  83.6 51.5 %reduce-scatter.5.cloned.1.call-done = f32[256,1280]{1,0:T(8,128)} async-done(((f32[1024,1280]{1,0:T(8,128)}), f32[256,1280]{1,0:T(8,128)}) %reduce-scatter.5.cloned.1.call-update) | async-done | bytes 1310736 | tf_op jit(solution)/shard_map/reduce_scatter | solution.py:111
  140.1 24.6 %all-gather.7.cloned.1.call-done = bf16[1024,1280]{1,0:T(8,128)(2,1)} async-done(((bf16[256,1280]{1,0:T(8,128)(2,1)}), bf16[1024,1280]{1,0:T(8,128)(2,1)}) %all-gather.7.cloned.1.call-update) | async-done | bytes 2621456 | tf_op jit(solution)/shard_map/all_gather | solution.py:120
  164.8 8.6 fusion.77
  173.4 18.5 %all-gather.9.cloned.1.call-done = bf16[1024,1280]{1,0:T(8,128)(2,1)} async-done(((bf16[256,1280]{1,0:T(8,128)(2,1)}), bf16[1024,1280]{1,0:T(8,128)(2,1)}) %all-gather.9.cloned.1.call-update) | async-done | bytes 2621456 | tf_op jit(solution)/shard_map/all_gather | solution.py:135
  191.8 18.3 %convert_reduce_fusion = (f32[1280]{0:T(1024)}, bf16[1024,1280]{1,0:T(8,128)(2,1)S(1)}, f32[1024,1280]{1,0:T(8,128)}) fusion(f32[1024,1280]{1,0:T(8,128)} %fusion.77, f32[1280]{0:T(1024)S(1)} %copy-done.48, bf16[1024,1280]{1,0:T(8,128)(2,1)} %all-gather.9.cloned.1.call-done, bf16[1280,1280]{1,0:T(8,128)(2,1)S(1)} %copy-done), kind=kOutput, calls=%fused_computation.51 | convolution fusion | flops 3453745920 | bytes 19015680 | tf_op jit(solution)/shard_map/rd,fd->rf/dot_general | solution.py:139
  211.7 5.3 fusion.78
  217.1 4.8 multiply_convert_fusion.1
  223.4 4.8 convolution_convert_fusion
  228.2 40.3 %reduce-scatter.9.cloned.1.call-done = f32[256,1280]{1,0:T(8,128)} async-done(((f32[1024,1280]{1,0:T(8,128)}), f32[256,1280]{1,0:T(8,128)}) %reduce-scatter.9.cloned.1.call-update) | async-done | bytes 1310736 | tf_op jit(solution)/shard_map/reduce_scatter | solution.py:149
  270.9 35.3 %reduce-scatter.7.cloned.1.call-done = bf16[256,1280]{1,0:T(8,128)(2,1)} async-done(((bf16[1024,1280]{1,0:T(8,128)(2,1)}), bf16[256,1280]{1,0:T(8,128)(2,1)}) %reduce-scatter.7.cloned.1.call-update) | async-done | bytes 655376 | tf_op jit(solution)/shard_map/reduce_scatter | solution.py:125
  306.3 3.0 fusion.73
  311.4 25.5 %all-gather.11.cloned.1.call-done = bf16[1024,1280]{1,0:T(8,128)(2,1)} async-done(((bf16[256,1280]{1,0:T(8,128)(2,1)}), bf16[1024,1280]{1,0:T(8,128)(2,1)}) %all-gather.11.cloned.1.call-update) | async-done | bytes 2621456 | tf_op jit(solution)/shard_map/all_gather | solution.py:160
  336.9 3.8 convolution_convert_fusion.1
  340.7 3.1 squeeze.50
  345.8 47.2 %while.48 = (s32[]{:T(128)}, f32[1024,5,64]{0,2,1:T(8,128)S(1)}, f32[1024,5,64]{0,2,1:T(8,128)}, bf16[2,512,5,64]{1,3,2,0:T(8,128)(2,1)}, bf16[2,512,5,64]{1,3,2...) while((s32[]{:T(128)}, f32[1024,5,64]{0,2,1:T(8,128)S(1)}, ...), condition=%wide.region_15.16_spmd.clone, body=%wide.region_13.15_spmd.clone.sunk | while | flops 1719007744 | bytes 176708368 | solution.py:70
  348.1 3.3 multiply_reduce_fusion.5
  351.4 4.3 multiply_convert_fusion.3
  355.8 3.8 fusion.142
  359.6 5.7 fusion.144
  365.3 3.4 fusion.143
  371.0 3.3 multiply_reduce_fusion.5
  374.3 4.3 multiply_convert_fusion.3
  378.6 3.8 fusion.142
  382.4 5.7 fusion.144
  388.1 4.8 fusion.143
  397.1 6.7 convolution_bitcast_fusion
  403.9 9.8 fusion.80
  413.7 5.6 fusion.81
  422.3 4.4 fusion.48
  428.3 37.2 %all-reduce.1 = (f32[2,320]{1,0:T(2,128)}, f32[1280]{0:T(1024)}) all-reduce(f32[2,320]{1,0:T(2,128)S(1)} %pad_maximum_fusion.3, f32[1280]{0:T(1024)S(1)} %copy-done.47), channel_id=1, replica_groups=mesh['dp'=8,'tensor'=4] {'dp'}, use_global_device_ids=true, to_apply=%region_26.27 | all-reduce | flops 1920 | bytes 15360 | tf_op jit(solution)/shard_map/psum | solution.py:199
  468.6 2.8 convert_reduce_fusion.2
  471.4 43.2 %all-reduce = (f32[1280]{0:T(1024)}, f32[1280]{0:T(1024)}, f32[1280]{0:T(1024)}, f32[1280]{0:T(1024)}, f32[1280]{0:T(1024)}, /*index=5*/f32[1280]{0:T(1024)}) all-reduce(f32[1280]{0:T(1024)S(1)} %get-tuple-element.217, f32[1280]{0:T(1024)S(1)} %get-tuple-element.220, ...), channel_id=1, replica_groups=mesh['dp'=8,'tensor'=4] {'dp','tensor'}, use_global_device_ids=true, to_apply=%region_20.21 | all-reduce | flops 7680 | bytes 61440 | tf_op jit(solution)/shard_map/psum | solution.py:211
  514.6 540.4 %all-reduce.5.cloned.1.call-done = (f32[1280,3,320]{0,2,1:T(8,128)}, f32[320,1280]{1,0:T(8,128)}, f32[1280,1280]{1,0:T(8,128)}, f32[1280,1280]{1,0:T(8,128)}) async-done(((f32[1280,3,320]{0,2,1:T(8,128)}, f32[320,1280]{1,0:T(8,128)}, f32[1280,1280]{1,0:T(8,128)}, f32[1280,1280]{1,0:T(8,128)}), (f32[1280,3,320]{0,2,1:T(8,128)}, f32[320,1280]{1,0:T(8,128)}, f32[1280,1280]{1,0:T(8,128)}, ...) | async-done | bytes 19660816 | tf_op jit(solution)/shard_map/psum | solution.py:199
  1055.0 5.4 copy.68
  1062.1 3.3 copy.70
  1066.4 3.3 copy.71
  (196 shorter events, 48.8 us)
Async XLA Ops:
  7.2 184.7 %copy-start = (bf16[1280,1280]{1,0:T(8,128)(2,1)S(1)}, bf16[1280,1280]{1,0:T(8,128)(2,1)}, u32[]{:S(2)}) copy-start(bf16[1280,1280]{1,0:T(8,128)(2,1)} %param.31) | copy-start | bytes 9830404
  7.2 6.4 copy-start.49
  7.2 34.7 %all-gather.5.cloned.1.call-start = ((), (), s32[]{:S(2)}) async-start(), calls=%async_computation.4 | async-start | bytes 3276800 | tf_op jit(solution)/shard_map/all_gather | solution.py:103
  13.5 121.6 %reduce-scatter.5.cloned.1.call-start = ((), (), s32[]{:S(2)}) async-start(), calls=%async_computation.5 | async-start | bytes 6553600 | tf_op jit(solution)/shard_map/reduce_scatter | solution.py:111
  83.5 51.6 %copy-start.44 = (f32[1280]{0:T(1024)S(1)}, f32[1280]{0:T(1024)}, u32[]{:S(2)}) copy-start(f32[1280]{0:T(1024)} %param.26) | copy-start | bytes 15364
  83.5 54.3 %copy-start.32 = (f32[1280]{0:T(1024)S(1)}, f32[1280]{0:T(1024)}, u32[]{:S(2)}) copy-start(f32[1280]{0:T(1024)} %param.27) | copy-start | bytes 15364
  83.5 54.3 %copy-start.45 = (f32[1280]{0:T(1024)S(1)}, f32[1280]{0:T(1024)}, u32[]{:S(2)}) copy-start(f32[1280]{0:T(1024)} %param.28) | copy-start | bytes 15364
  83.6 81.2 %all-gather.7.cloned.1.call-start = ((), (), s32[]{:S(2)}) async-start(), calls=%async_computation.6 | async-start | bytes 3276800 | tf_op jit(solution)/shard_map/all_gather | solution.py:120
  139.0 52.8 %all-gather.9.cloned.1.call-start = ((), (), s32[]{:S(2)}) async-start(), calls=%async_computation.8 | async-start | bytes 3276800 | tf_op jit(solution)/shard_map/all_gather | solution.py:135
  139.6 52.2 %copy-start.48 = (f32[1280]{0:T(1024)S(1)}, f32[1280]{0:T(1024)}, u32[]{:S(2)}) copy-start(f32[1280]{0:T(1024)} %param.30) | copy-start | bytes 15364
  139.6 128.9 %reduce-scatter.9.cloned.1.call-start = ((), (), s32[]{:S(2)}) async-start(), calls=%async_computation.9 | async-start | bytes 6553600 | tf_op jit(solution)/shard_map/reduce_scatter | solution.py:149
  191.8 19.8 %copy-start.50 = (bf16[1280,1280]{1,0:T(8,128)(2,1)S(1)}, bf16[1280,1280]{1,0:T(8,128)(2,1)}, u32[]{:S(2)}) copy-start(bf16[1280,1280]{1,0:T(8,128)(2,1)} %param.29) | copy-start | bytes 9830404
  217.0 89.2 %reduce-scatter.7.cloned.1.call-start = ((), (), s32[]{:S(2)}) async-start(), calls=%async_computation.7 | async-start | bytes 3276800 | tf_op jit(solution)/shard_map/reduce_scatter | solution.py:125
  228.1 40.4 %copy-start.7 = (f32[256,1280]{1,0:T(8,128)S(1)}, f32[256,1280]{1,0:T(8,128)}, u32[]{:S(2)}) copy-start(f32[256,1280]{1,0:T(8,128)} %copy-done.6) | copy-start | bytes 3932164
  228.1 78.1 %copy-start.46 = (f32[1280]{0:T(1024)S(1)}, f32[1280]{0:T(1024)}, u32[]{:S(2)}) copy-start(f32[1280]{0:T(1024)} %param.32) | copy-start | bytes 15364
  228.2 108.7 %all-gather.11.cloned.1.call-start = ((), (), s32[]{:S(2)}) async-start(), calls=%async_computation.10 | async-start | bytes 3276800 | tf_op jit(solution)/shard_map/all_gather | solution.py:160
  270.9 38.3 %copy-start.17 = (bf16[256,1280]{1,0:T(8,128)(2,1)S(1)}, bf16[256,1280]{1,0:T(8,128)(2,1)}, u32[]{:S(2)}) copy-start(bf16[256,1280]{1,0:T(8,128)(2,1)} %param.33) | copy-start | bytes 1966084
  309.3 27.6 %copy-start.11 = (f32[256,1280]{1,0:T(8,128)}, f32[256,1280]{1,0:T(8,128)S(1)}, u32[]{:S(2)}) copy-start(f32[256,1280]{1,0:T(8,128)S(1)} %get-tuple-element.278) | copy-start | bytes 3932164
  311.2 154.4 %reduce-scatter.11.cloned.1.call-start = ((), (), s32[]{:S(2)}) async-start(), calls=%async_computation.11 | async-start | bytes 6553600 | tf_op jit(solution)/shard_map/reduce_scatter | solution.py:183
  340.7 5.1 copy-start.4
  340.7 5.1 copy-start.5
  340.7 5.1 copy-start.10
  347.4 4.0 copy-start.2
  355.7 9.5 copy-start.3
  359.5 5.7 copy-start.15
  370.3 4.0 copy-start.2
  378.6 9.5 copy-start.3
  382.4 5.7 copy-start.15
  394.5 9.3 copy-start.27
  397.0 6.8 copy-start.25
  397.1 6.7 copy-start.29
  403.9 9.9 copy-start.22
  403.9 651.1 %all-reduce.5.cloned.1.call-start = ((), (), s32[]{:S(2)}) async-start(), calls=%async_computation.12 | async-start | bytes 39321600 | tf_op jit(solution)/shard_map/psum | solution.py:199
  403.9 9.8 copy-start.52
  413.7 5.6 copy-start.20
  413.7 5.6 copy-start.53
  426.7 38.9 %copy-start.8 = (bf16[256,1280]{1,0:T(8,128)(2,1)S(1)}, bf16[256,1280]{1,0:T(8,128)(2,1)}, u32[]{:S(2)}) copy-start(bf16[256,1280]{1,0:T(8,128)(2,1)} %param.19) | copy-start | bytes 1966084
  426.7 38.9 %copy-start.31 = (f32[1280]{0:T(1024)S(1)}, f32[1280]{0:T(1024)}, u32[]{:S(2)}) copy-start(f32[1280]{0:T(1024)} %param.21) | copy-start | bytes 15364
  426.7 38.9 %copy-start.34 = (f32[256]{0:T(256)S(1)}, f32[256]{0:T(256)}, u32[]{:S(2)}) copy-start(f32[256]{0:T(256)} %copy-done.33) | copy-start | bytes 3076
  426.7 41.0 %copy-start.43 = (f32[256]{0:T(256)S(1)}, f32[256]{0:T(256)}, u32[]{:S(2)}) copy-start(f32[256]{0:T(256)} %copy-done.42) | copy-start | bytes 3076
  426.7 41.0 %copy-start.39 = (f32[256]{0:T(256)S(1)}, f32[256]{0:T(256)}, u32[]{:S(2)}) copy-start(f32[256]{0:T(256)} %copy-done.38) | copy-start | bytes 3076
  426.7 41.8 %copy-start.12 = (f32[256,1280]{1,0:T(8,128)S(1)}, f32[256,1280]{1,0:T(8,128)}, u32[]{:S(2)}) copy-start(f32[256,1280]{1,0:T(8,128)} %copy-done.11) | copy-start | bytes 3932164
  426.8 41.8 %copy-start.41 = (f32[256]{0:T(256)S(1)}, f32[256]{0:T(256)}, u32[]{:S(2)}) copy-start(f32[256]{0:T(256)} %copy-done.40) | copy-start | bytes 3076
  1055.0 5.4 copy-start.23
  1055.0 7.2 copy-start.16
  1060.3 5.1 slice-start
  1062.1 4.3 slice-start.1
  1066.4 4.3 copy-start.1
  (23 other events, 47.0 us)
Sparse Core Ops, SparseCore 0:
  13.6 28.2 all-gather.4
  83.7 51.3 reduce-scatter.4
  139.2 25.5 all-gather.6
  166.2 25.5 all-gather.8
  217.1 51.3 reduce-scatter.8
  271.5 34.6 reduce-scatter.6
  311.3 25.5 all-gather.10
  404.0 51.3 reduce-scatter.10
  461.3 593.6 all-reduce.4
where the time goes:
time: 1090 us; the launch traced here: 1080 us
  waiting for transfers between devices  765 us (70%)
  matrix products  129 us (12%)
  blocking collectives  80.4 us (7%)
  other arithmetic  48.6 us (4%)
  local copies, waits for them, and re-layouts  38.2 us (4%)
  between operations  14.8 us (1%)
    psum x1, waiting for transfers between devices, local(): lax.psum((grad_weight_in, grad_bias_in, grad_weight_out, grad_weight_up,...  540 us
    reduce_scatter x1, waiting for transfers between devices, local(): lax.psum_scatter(jnp.dot(context_rows, weight_out, preferred_element_type...  51.5 us
    psum x1, blocking collectives, local(): lax.psum((grad_gain_one, grad_shift_one, grad_bias_out, grad_gain_two, gr...  43.2 us
    reduce_scatter x1, waiting for transfers between devices, local(): lax.psum_scatter(jnp.einsum('rf,df->rd', grad_hidden, weight_up, preferre...  40.3 us
    psum x1, blocking collectives, local(): lax.psum((grad_weight_in, grad_bias_in, grad_weight_out, grad_weight_up,...  37.2 us
    reduce_scatter x1, waiting for transfers between devices, local(): lax.psum_scatter(jnp.dot(active, weight_down, preferred_element_type=jnp....  35.3 us
    all_gather x1, waiting for transfers between devices, local(): first = lax.all_gather(first_local, 'tensor', axis=0, tiled=True)  28.2 us
    all_gather x1, waiting for transfers between devices, local(): branch_group = lax.all_gather(grad_branch, 'tensor', axis=0, tiled=True)  25.5 us
  transfers between devices with their start and end apart: 9, of which 8 were waited for; matrix products, arithmetic and copies ran while one was open for 5% of the time, Pallas kernels for 0%

commit v1 on v0

--- a/solution.py
+++ b/solution.py
@@ -71,6 +71,10 @@
         step, (zero_state, zero_state), (query_seq, grad_seq, log_seq)
     )
     return (query_grads, key_total.astype(jnp.bfloat16), value_total.astype(jnp.bfloat16))
+
+
+def sum_dp(part):
+    return lax.psum(part.astype(jnp.bfloat16), "dp").astype(jnp.float32)
 
 
 def local(
@@ -109,11 +113,11 @@
     context_rows = context.reshape(group_rows, width).astype(jnp.bfloat16)
     middle = rows_in + (
         lax.psum_scatter(
-            jnp.dot(context_rows, weight_out, preferred_element_type=jnp.float32),
+            jnp.dot(context_rows, weight_out, preferred_element_type=jnp.float32).astype(jnp.bfloat16),
             "tensor",
             scatter_dimension=0,
             tiled=True,
-        )
+        ).astype(jnp.float32)
         + bias_out
     )
     second_local = normalize(middle, gain_two, shift_two).astype(jnp.bfloat16)
@@ -147,11 +151,11 @@
     )
     grad_bias_up = jnp.sum(grad_hidden.astype(jnp.float32), axis=0)
     grad_second = lax.psum_scatter(
-        jnp.einsum("rf,df->rd", grad_hidden, weight_up, preferred_element_type=jnp.float32),
+        jnp.einsum("rf,df->rd", grad_hidden, weight_up, preferred_element_type=jnp.float32).astype(jnp.bfloat16),
         "tensor",
         scatter_dimension=0,
         tiled=True,
-    )
+    ).astype(jnp.float32)
     unused_two, second_pull = jax.vjp(normalize, middle, gain_two, shift_two)
     middle_part, grad_gain_two, grad_shift_two = second_pull(grad_second)
     grad_middle = grad_out + middle_part
@@ -181,32 +185,19 @@
         ]
     )
     grad_first = lax.psum_scatter(
-        jnp.einsum("rcw,dcw->rd", grad_mixed, weight_in, preferred_element_type=jnp.float32),
+        jnp.einsum("rcw,dcw->rd", grad_mixed, weight_in, preferred_element_type=jnp.float32).astype(jnp.bfloat16),
         "tensor",
         scatter_dimension=0,
         tiled=True,
-    )
+    ).astype(jnp.float32)
     unused_one, first_pull = jax.vjp(normalize, rows_in, gain_one, shift_one)
     rows_part, grad_gain_one, grad_shift_one = first_pull(grad_first)
     grad_tokens = grad_middle + rows_part
-    (
-        grad_weight_in,
-        grad_bias_in,
-        grad_weight_out,
-        grad_weight_up,
-        grad_bias_up,
-        grad_weight_down,
-    ) = lax.psum(
-        (
-            grad_weight_in,
-            grad_bias_in,
-            grad_weight_out,
-            grad_weight_up,
-            grad_bias_up,
-            grad_weight_down,
-        ),
-        "dp",
-    )
+    grad_bias_in, grad_bias_up = lax.psum((grad_bias_in, grad_bias_up), "dp")
+    grad_weight_in = sum_dp(grad_weight_in)
+    grad_weight_out = sum_dp(grad_weight_out)
+    grad_weight_up = sum_dp(grad_weight_up)
+    grad_weight_down = sum_dp(grad_weight_down)
     grad_gain_one, grad_shift_one, grad_bias_out, grad_gain_two, grad_shift_two, grad_bias_down = (
         lax.psum(
             (

time: 1090 us -> 735 us (0.67)
  waiting for transfers between devices: 765 us -> 435 us
  matrix products: 129 us -> 109 us
  local copies, waits for them, and re-layouts: 38.2 us -> 27.2 us
    psum x1, waiting for transfers between devices: 540 us -> 244 us  [sum_dp(): return lax.psum(part.astype(jnp.bfloat16), 'dp').astype(jnp.float32)]
    reduce_scatter x1, waiting for transfers between devices: 40.3 us -> 23.6 us  [local(): lax.psum_scatter(jnp.einsum('rf,df->rd', grad_hidden, weight_up, preferre...]
    reduce_scatter x1, waiting for transfers between devices: 51.5 us -> 34.8 us  [local(): lax.psum_scatter(jnp.dot(context_rows, weight_out, preferred_element_type...]
    unnamed x110, local copies, waits for them, and re-layouts: 24.6 us -> 12 us
    convert_element_type x0 -> x4, other arithmetic: none -> 11.9 us  [sum_dp(): return lax.psum(part.astype(jnp.bfloat16), 'dp').astype(jnp.float32)]
  transfers between devices with their start and end apart: 9 -> 9, of which waited for: 8 -> 8; matrix products, arithmetic and copies ran while one was open for 5% -> 6% of each run, Pallas kernels for 0% -> 0%
where the time goes in v1:
time: 735 us; the launch traced here: 726 us
  waiting for transfers between devices  435 us (59%)
  matrix products  109 us (15%)
  blocking collectives  81.5 us (11%)
  other arithmetic  57.4 us (8%)
  local copies, waits for them, and re-layouts  27.2 us (4%)
  between operations  14.5 us (2%)
    psum x1, waiting for transfers between devices, sum_dp(): return lax.psum(part.astype(jnp.bfloat16), 'dp').astype(jnp.float32)  244 us
    psum x1, blocking collectives, local(): lax.psum((grad_gain_one, grad_shift_one, grad_bias_out, grad_gain_two, gr...  43.9 us
    psum x1, blocking collectives, local(): grad_bias_in, grad_bias_up = lax.psum((grad_bias_in, grad_bias_up), 'dp')  37.6 us
    reduce_scatter x1, waiting for transfers between devices, local(): lax.psum_scatter(jnp.dot(active, weight_down, preferred_element_type=jnp....  35.3 us
    reduce_scatter x1, waiting for transfers between devices, local(): lax.psum_scatter(jnp.dot(context_rows, weight_out, preferred_element_type...  34.8 us
    all_gather x1, waiting for transfers between devices, local(): first = lax.all_gather(first_local, 'tensor', axis=0, tiled=True)  28.2 us
    all_gather x1, waiting for transfers between devices, local(): branch_group = lax.all_gather(grad_branch, 'tensor', axis=0, tiled=True)  25.2 us
    all_gather x1, waiting for transfers between devices, local(): second = lax.all_gather(second_local, 'tensor', axis=0, tiled=True)  24.9 us
  transfers between devices with their start and end apart: 9, of which 8 were waited for; matrix products, arithmetic and copies ran while one was open for 6% of the time, Pallas kernels for 0%

profile of v1, /device:TPU:0, one launch (start us, length us, event | category | flops | bytes accessed | tf_op | source)
XLA Modules:
  0.0 726.3 jit_solution(13957968241348811471)
XLA Ops:
  11.2 2.3 fusion.60
  13.8 28.2 %all-gather.5.cloned.1.call-done = bf16[1024,1280]{1,0:T(8,128)(2,1)} async-done(((bf16[256,1280]{1,0:T(8,128)(2,1)}), bf16[1024,1280]{1,0:T(8,128)(2,1)}) %all-gather.5.cloned.1.call-update) | async-done | bytes 2621456 | tf_op jit(solution)/shard_map/all_gather | solution.py:107
  41.9 5.2 fusion.49
  49.7 3.2 squeeze.48
  52.9 2.4 add_convert_fusion.2
  56.4 21.0 %while.47 = (s32[]{:T(128)}, bf16[2,512,5,64]{1,3,2,0:T(8,128)(2,1)}, f32[2,5,512]{2,1,0:T(8,128)S(1)}, s32[]{:T(128)}, bf16[2,512,5,64]{1,3,2,0:T(8,128)(2,1)},...) while((s32[]{:T(128)}, bf16[2,512,5,64]{1,3,2,0:T(8,128)(2,1)}, ...), condition=%wide.region_5.6_spmd, body=%wide.region_2.5_spmd.sunk | while | flops 702544384 | bytes 41732288 | solution.py:36
  57.1 2.9 fusion.127
  60.0 2.5 fusion.128
  62.5 3.6 fusion.129
  67.6 2.9 fusion.127
  70.5 2.5 fusion.128
  73.0 3.6 fusion.129
  80.3 3.1 convolution_convert_fusion.4
  83.4 34.8 %reduce-scatter.5.cloned.1.call-done = bf16[256,1280]{1,0:T(8,128)(2,1)} async-done(((bf16[1024,1280]{1,0:T(8,128)(2,1)}), bf16[256,1280]{1,0:T(8,128)(2,1)}) %reduce-scatter.5.cloned.1.call-update) | async-done | bytes 655376 | tf_op jit(solution)/shard_map/reduce_scatter | solution.py:115
  123.7 24.9 %all-gather.7.cloned.1.call-done = bf16[1024,1280]{1,0:T(8,128)(2,1)} async-done(((bf16[256,1280]{1,0:T(8,128)(2,1)}), bf16[1024,1280]{1,0:T(8,128)(2,1)}) %all-gather.7.cloned.1.call-update) | async-done | bytes 2621456 | tf_op jit(solution)/shard_map/all_gather | solution.py:124
  148.6 8.6 %fusion.79 = f32[1024,1280]{1,0:T(8,128)} fusion(bf16[1024,1280]{1,0:T(8,128)(2,1)} %all-gather.7.cloned.1.call-done, bf16[1280,1280]{1,0:T(8,128)(2,1)} %param.29), kind=kOutput, calls=%fused_computation.140 | convolution fusion | flops 3355443200 | bytes 11141120 | tf_op jit(solution)/shard_map/dot_general | solution.py:125
  157.2 18.5 %all-gather.9.cloned.1.call-done = bf16[1024,1280]{1,0:T(8,128)(2,1)} async-done(((bf16[256,1280]{1,0:T(8,128)(2,1)}), bf16[1024,1280]{1,0:T(8,128)(2,1)}) %all-gather.9.cloned.1.call-update) | async-done | bytes 2621456 | tf_op jit(solution)/shard_map/all_gather | solution.py:139
  175.7 18.3 %convert_reduce_fusion = (f32[1280]{0:T(1024)}, bf16[1024,1280]{1,0:T(8,128)(2,1)S(1)}, f32[1024,1280]{1,0:T(8,128)}) fusion(f32[1024,1280]{1,0:T(8,128)} %fusion.79, f32[1280]{0:T(1024)S(1)} %copy-done.51, bf16[1024,1280]{1,0:T(8,128)(2,1)} %all-gather.9.cloned.1.call-done, bf16[1280,1280]{1,0:T(8,128)(2,1)S(1)} %copy-done), kind=kOutput, calls=%fused_computation.54 | convolution fusion | flops 3453745920 | bytes 19015680 | tf_op jit(solution)/shard_map/rd,fd->rf/dot_general | solution.py:143
  195.5 4.8 convolution_convert_fusion.2
  200.4 4.8 multiply_convert_fusion.1
  206.8 4.8 convolution_convert_fusion.3
  211.6 23.6 %reduce-scatter.9.cloned.1.call-done = bf16[256,1280]{1,0:T(8,128)(2,1)} async-done(((bf16[1024,1280]{1,0:T(8,128)(2,1)}), bf16[256,1280]{1,0:T(8,128)(2,1)}) %reduce-scatter.9.cloned.1.call-update) | async-done | bytes 655376 | tf_op jit(solution)/shard_map/reduce_scatter | solution.py:153
  235.2 2.3 fusion.64
  237.5 35.3 %reduce-scatter.7.cloned.1.call-done = bf16[256,1280]{1,0:T(8,128)(2,1)} async-done(((bf16[1024,1280]{1,0:T(8,128)(2,1)}), bf16[256,1280]{1,0:T(8,128)(2,1)}) %reduce-scatter.7.cloned.1.call-update) | async-done | bytes 655376 | tf_op jit(solution)/shard_map/reduce_scatter | solution.py:129
  272.8 3.0 fusion.77
  278.3 25.2 %all-gather.11.cloned.1.call-done = bf16[1024,1280]{1,0:T(8,128)(2,1)} async-done(((bf16[256,1280]{1,0:T(8,128)(2,1)}), bf16[1024,1280]{1,0:T(8,128)(2,1)}) %all-gather.11.cloned.1.call-update) | async-done | bytes 2621456 | tf_op jit(solution)/shard_map/all_gather | solution.py:164
  303.5 3.8 convolution_convert_fusion.7
  307.3 3.1 squeeze.50
  310.4 2.0 copy.34
  312.4 31.3 %while.48 = (s32[]{:T(128)}, f32[1024,5,64]{0,2,1:T(8,128)S(1)}, f32[1024,5,64]{0,2,1:T(8,128)}, bf16[2,512,5,64]{1,3,2,0:T(8,128)(2,1)}, bf16[2,512,5,64]{1,3,2...) while((s32[]{:T(128)}, f32[1024,5,64]{0,2,1:T(8,128)S(1)}, ...), condition=%wide.region_15.16_spmd.clone, body=%wide.region_13.15_spmd.clone.sunk | while | flops 1719007744 | bytes 95443200 | solution.py:70
  314.7 3.5 fusion.141
  318.2 3.3 multiply_reduce_fusion.3
  321.4 3.0 multiply_convert_fusion.3
  329.6 4.8 fusion.141
  334.4 3.3 multiply_reduce_fusion.3
  337.7 3.0 multiply_convert_fusion.3
  343.9 2.0 copy.35
  348.6 5.9 bitcast_convert_fusion
  356.3 6.9 convolution_convert_fusion
  363.2 5.0 convolution_convert_fusion.1
  370.7 3.9 convolution_convert_fusion.5
  376.0 37.6 %all-reduce.1 = (f32[2,320]{1,0:T(2,128)}, f32[1280]{0:T(1024)}) all-reduce(f32[2,320]{1,0:T(2,128)S(1)} %pad_maximum_fusion.3, f32[1280]{0:T(1024)S(1)} %copy-done.50), channel_id=1, replica_groups=mesh['dp'=8,'tensor'=4] {'dp'}, use_global_device_ids=true, to_apply=%region_26.27 | all-reduce | flops 1920 | bytes 15360 | tf_op jit(solution)/shard_map/psum | solution.py:196
  419.0 43.9 %all-reduce = (f32[1280]{0:T(1024)}, f32[1280]{0:T(1024)}, f32[1280]{0:T(1024)}, f32[1280]{0:T(1024)}, f32[1280]{0:T(1024)}, /*index=5*/f32[1280]{0:T(1024)}) all-reduce(f32[1280]{0:T(1024)S(1)} %get-tuple-element.217, f32[1280]{0:T(1024)S(1)} %get-tuple-element.220, ...), channel_id=1, replica_groups=mesh['dp'=8,'tensor'=4] {'dp','tensor'}, use_global_device_ids=true, to_apply=%region_20.21 | all-reduce | flops 7680 | bytes 61440 | tf_op jit(solution)/shard_map/psum | solution.py:202
  462.8 244.3 %all-reduce.5.cloned.1.call-done = (bf16[1280,3,320]{0,2,1:T(8,128)(2,1)}, bf16[320,1280]{1,0:T(8,128)(2,1)}, bf16[1280,1280]{1,0:T(8,128)(2,1)}, bf16[1280,1280]{1,0:T(8,128)(2,1)}) async-done(((bf16[1280,3,320]{0,2,1:T(8,128)(2,1)}, bf16[320,1280]{1,0:T(8,128)(2,1)}, bf16[1280,1280]{1,0:T(8,128)(2,1)}, bf16[1280,1280]{1,0:T(8,128)(2,1)}), (bf16[1280,3,320]{0,2,1:T(8,128)(2,1)}, ...) | async-done | bytes 9830416 | tf_op jit(solution)/shard_map/psum | solution.py:77
  707.1 2.6 convert_element_type.156
  709.7 2.7 convert_element_type.152
  713.0 3.3 convert_element_type.159
  716.3 3.3 convert_element_type.162
  (203 shorter events, 49.2 us)
Async XLA Ops:
  7.2 168.5 %copy-start = (bf16[1280,1280]{1,0:T(8,128)(2,1)S(1)}, bf16[1280,1280]{1,0:T(8,128)(2,1)}, u32[]{:S(2)}) copy-start(bf16[1280,1280]{1,0:T(8,128)(2,1)} %param.31) | copy-start | bytes 9830404
  7.2 6.4 copy-start.52
  7.2 34.7 %all-gather.5.cloned.1.call-start = ((), (), s32[]{:S(2)}) async-start(), calls=%async_computation.4 | async-start | bytes 3276800 | tf_op jit(solution)/shard_map/all_gather | solution.py:107
  13.5 104.7 %reduce-scatter.5.cloned.1.call-start = ((), (), s32[]{:S(2)}) async-start(), calls=%async_computation.5 | async-start | bytes 3276800 | tf_op jit(solution)/shard_map/reduce_scatter | solution.py:115
  60.0 2.5 copy-start.7
  77.5 2.8 copy-start.57
  83.4 34.9 %copy-start.34 = (f32[1280]{0:T(1024)S(1)}, f32[1280]{0:T(1024)}, u32[]{:S(2)}) copy-start(f32[1280]{0:T(1024)} %param.26) | copy-start | bytes 15364
  83.4 38.2 %copy-start.36 = (f32[1280]{0:T(1024)S(1)}, f32[1280]{0:T(1024)}, u32[]{:S(2)}) copy-start(f32[1280]{0:T(1024)} %param.27) | copy-start | bytes 15364
  83.4 38.2 %copy-start.48 = (f32[1280]{0:T(1024)S(1)}, f32[1280]{0:T(1024)}, u32[]{:S(2)}) copy-start(f32[1280]{0:T(1024)} %param.28) | copy-start | bytes 15364
  83.4 65.2 %all-gather.7.cloned.1.call-start = ((), (), s32[]{:S(2)}) async-start(), calls=%async_computation.6 | async-start | bytes 3276800 | tf_op jit(solution)/shard_map/all_gather | solution.py:124
  118.2 3.4 copy-start.3
  118.2 3.4 copy-start.9
  122.9 52.8 %all-gather.9.cloned.1.call-start = ((), (), s32[]{:S(2)}) async-start(), calls=%async_computation.8 | async-start | bytes 3276800 | tf_op jit(solution)/shard_map/all_gather | solution.py:139
  123.5 52.2 %copy-start.51 = (f32[1280]{0:T(1024)S(1)}, f32[1280]{0:T(1024)}, u32[]{:S(2)}) copy-start(f32[1280]{0:T(1024)} %param.30) | copy-start | bytes 15364
  123.5 111.7 %reduce-scatter.9.cloned.1.call-start = ((), (), s32[]{:S(2)}) async-start(), calls=%async_computation.9 | async-start | bytes 3276800 | tf_op jit(solution)/shard_map/reduce_scatter | solution.py:153
  175.7 19.8 %copy-start.53 = (bf16[1280,1280]{1,0:T(8,128)(2,1)S(1)}, bf16[1280,1280]{1,0:T(8,128)(2,1)}, u32[]{:S(2)}) copy-start(bf16[1280,1280]{1,0:T(8,128)(2,1)} %param.29) | copy-start | bytes 9830404
  200.3 72.5 %reduce-scatter.7.cloned.1.call-start = ((), (), s32[]{:S(2)}) async-start(), calls=%async_computation.7 | async-start | bytes 3276800 | tf_op jit(solution)/shard_map/reduce_scatter | solution.py:129
  211.5 23.6 %copy-start.4 = (bf16[256,1280]{1,0:T(8,128)(2,1)S(1)}, bf16[256,1280]{1,0:T(8,128)(2,1)}, u32[]{:S(2)}) copy-start(bf16[256,1280]{1,0:T(8,128)(2,1)} %param.19) | copy-start | bytes 1966084
  211.5 23.6 %copy-start.10 = (bf16[256,1280]{1,0:T(8,128)(2,1)S(1)}, bf16[256,1280]{1,0:T(8,128)(2,1)}, u32[]{:S(2)}) copy-start(bf16[256,1280]{1,0:T(8,128)(2,1)} %reduce-scatter.5.cloned.1.call-done) | copy-start | bytes 1966084
  211.6 61.3 %copy-start.49 = (f32[1280]{0:T(1024)S(1)}, f32[1280]{0:T(1024)}, u32[]{:S(2)}) copy-start(f32[1280]{0:T(1024)} %param.32) | copy-start | bytes 15364
  211.6 91.9 %all-gather.11.cloned.1.call-start = ((), (), s32[]{:S(2)}) async-start(), calls=%async_computation.10 | async-start | bytes 3276800 | tf_op jit(solution)/shard_map/all_gather | solution.py:164
  237.5 38.3 %copy-start.14 = (bf16[256,1280]{1,0:T(8,128)(2,1)S(1)}, bf16[256,1280]{1,0:T(8,128)(2,1)}, u32[]{:S(2)}) copy-start(bf16[256,1280]{1,0:T(8,128)(2,1)} %param.33) | copy-start | bytes 1966084
  275.9 27.6 %copy-start.11 = (f32[256,1280]{1,0:T(8,128)}, f32[256,1280]{1,0:T(8,128)S(1)}, u32[]{:S(2)}) copy-start(f32[256,1280]{1,0:T(8,128)S(1)} %get-tuple-element.278) | copy-start | bytes 3932164
  277.8 135.9 %reduce-scatter.11.cloned.1.call-start = ((), (), s32[]{:S(2)}) async-start(), calls=%async_computation.11 | async-start | bytes 3276800 | tf_op jit(solution)/shard_map/reduce_scatter | solution.py:187
  307.3 5.1 copy-start.2
  307.3 5.1 copy-start.6
  307.3 5.1 copy-start.8
  321.4 3.0 copy-start.20
  337.7 3.0 copy-start.20
  343.9 4.0 copy-start.30
  354.6 352.6 %all-reduce.5.cloned.1.call-start = ((), (), s32[]{:S(2)}) async-start(), calls=%async_computation.12 | async-start | bytes 19660800 | tf_op jit(solution)/shard_map/psum | solution.py:77
  356.3 6.9 copy-start.55
  356.3 6.9 copy-start.59
  363.2 5.0 copy-start.27
  363.2 5.0 copy-start.56
  374.6 39.1 %copy-start.5 = (bf16[256,1280]{1,0:T(8,128)(2,1)S(1)}, bf16[256,1280]{1,0:T(8,128)(2,1)}, u32[]{:S(2)}) copy-start(bf16[256,1280]{1,0:T(8,128)(2,1)} %param.19) | copy-start | bytes 1966084
  374.6 39.1 %copy-start.35 = (f32[1280]{0:T(1024)S(1)}, f32[1280]{0:T(1024)}, u32[]{:S(2)}) copy-start(f32[1280]{0:T(1024)} %param.21) | copy-start | bytes 15364
  374.6 39.1 %copy-start.38 = (f32[256]{0:T(256)S(1)}, f32[256]{0:T(256)}, u32[]{:S(2)}) copy-start(f32[256]{0:T(256)} %copy-done.37) | copy-start | bytes 3076
  374.6 40.7 %copy-start.47 = (f32[256]{0:T(256)S(1)}, f32[256]{0:T(256)}, u32[]{:S(2)}) copy-start(f32[256]{0:T(256)} %copy-done.46) | copy-start | bytes 3076
  374.6 40.7 %copy-start.43 = (f32[256]{0:T(256)S(1)}, f32[256]{0:T(256)}, u32[]{:S(2)}) copy-start(f32[256]{0:T(256)} %copy-done.42) | copy-start | bytes 3076
  375.7 41.5 %copy-start.12 = (f32[256,1280]{1,0:T(8,128)S(1)}, f32[256,1280]{1,0:T(8,128)}, u32[]{:S(2)}) copy-start(f32[256,1280]{1,0:T(8,128)} %copy-done.11) | copy-start | bytes 3932164
  375.7 41.5 %copy-start.15 = (bf16[256,1280]{1,0:T(8,128)(2,1)S(1)}, bf16[256,1280]{1,0:T(8,128)(2,1)}, u32[]{:S(2)}) copy-start(bf16[256,1280]{1,0:T(8,128)(2,1)} %param.33) | copy-start | bytes 1966084
  375.7 41.5 %copy-start.45 = (f32[256]{0:T(256)S(1)}, f32[256]{0:T(256)}, u32[]{:S(2)}) copy-start(f32[256]{0:T(256)} %copy-done.44) | copy-start | bytes 3076
  413.7 3.5 copy-start.16
  707.1 2.6 copy-start.25
  709.7 3.3 copy-start.19
  713.0 3.3 copy-start.18
  716.3 3.3 copy-start.1
  (27 other events, 43.5 us)
Sparse Core Ops, SparseCore 0:
  13.6 28.2 all-gather.4
  83.5 34.6 reduce-scatter.4
  123.0 25.5 all-gather.6
  150.1 25.5 all-gather.8
  200.5 34.6 reduce-scatter.8
  238.2 34.6 reduce-scatter.6
  277.9 25.5 all-gather.10
  354.7 34.6 reduce-scatter.10
  395.0 312.0 all-reduce.4
